TPU v7x, 32 devices: a whole 2x2x4 slice. The times are simulated.
32 devices in a mesh: groups: 2 (over x), ex: 4 (over y, core), layer: 4 (over z).
Axes of the slice: x: 2, y: 2, z: 4, core: 2. Of those that a mesh axis runs over, the one named last changes fastest.
Arguments:
- query_grads: bfloat16 [4, 256, 4096], P('layer', 'ex')
- train_grads: bfloat16 [4, 4096, 4096], P('layer', ('groups', 'ex')), parts along dimension 1
- panels: bfloat16 [4, 4096, 4096], P('layer', 'ex'), as said below
- counts: int32 [8], P(('groups', 'ex')), parts along dimension 0, may hold values from 128 to 512, as said below
Outputs:
- scores: float32 [256, 4096], P('layer', ('groups', 'ex')), parts along dimension 1
There are 2 independent parts, one for each index of `groups`. A program takes and returns all parts, laid end to end along the dimension named above; an argument that names none is the same for every part. Nothing has to cross between parts.
Inputs may be any that keep to these rules, and one draw needn't show every extreme that they name: `counts`: each device's count lies between 128 and 512; in every draw some device has exactly 512 live examples. `panels`: each panel is symmetric.
All inputs are finite; a program needn't handle non-finite values.
Results may differ from a plain program's by a relative error of at most 0.0029.
Values may be sent and summed in bfloat16 or wider, within the bound.
A program may use at most 64 MiB of HBM per device.

v0:
```python
import math

import jax
import jax.numpy as jnp
from jax import lax
from jax.sharding import PartitionSpec as P


def per_device(query_grads, train_grads, panels, counts):
    train_rows = train_grads[0]
    panel_rows = panels[0]
    column_part = lax.dot_general(
        lax.all_gather(query_grads, "ex", axis=1, tiled=True)[0],
        panel_rows,
        (((1,), (1,)), ((), ())),
        preferred_element_type=jnp.float32,
    ).astype(jnp.bfloat16)
    partial_scores = lax.dot_general(
        lax.all_gather(column_part, "ex", axis=1, tiled=True),
        train_rows,
        (((1,), (1,)), ((), ())),
        preferred_element_type=jnp.float32,
    )
    alive_mask = (lax.iota(jnp.int32, train_rows.shape[0]) < counts[0]).astype(jnp.float32)
    partial_scores = partial_scores * alive_mask[None, :]
    summed = lax.psum_scatter(partial_scores, "layer", scatter_dimension=0, tiled=True)
    factor = 1.0 / math.sqrt(lax.axis_size("layer") * panel_rows.shape[1])
    return summed * factor


def solution(mesh):
    in_specs = (
        P("layer", "ex", None),
        P("layer", ("groups", "ex"), None),
        P("layer", "ex", None),
        P(("groups", "ex")),
    )
    out_specs = P("layer", ("groups", "ex"))
    return jax.shard_map(
        per_device, mesh=mesh, in_specs=in_specs, out_specs=out_specs, check_vma=False
    )
```

profile of v0, /device:TPU:0, one launch (start us, length us, event | category | flops | bytes accessed | tf_op | source)
XLA Modules:
  0.0 99.0 jit_solution(6862341524580495421)
XLA Ops:
  6.5 0.0 all-gather.3.cloned.1.call-start
  6.5 0.7 all-gather.3.cloned.1.call-update
  7.3 0.0 all-gather.5.cloned.1.call-start
  7.3 26.9 %all-gather.3.cloned.1.call-done = bf16[1,256,4096]{2,1,0:T(8,128)(2,1)} async-done(((bf16[1,64,4096]{2,1,0:T(8,128)(2,1)}), bf16[1,256,4096]{2,1,0:T(8,128)(2,1)}) %all-gather.3.cloned.1.call-update) | async-done | bytes 2097168 | tf_op jit(solution)/shard_map/all_gather | solution.py:13
  34.2 7.2 %fusion.5 = bf16[256,1024]{1,0:T(8,128)(2,1)} fusion(bf16[1,1024,4096]{2,1,0:T(8,128)(2,1)} %param.6, bf16[1,256,4096]{2,1,0:T(8,128)(2,1)} %all-gather.3.cloned.1.call-done), kind=kOutput, calls=%fused_computation.5 | convolution fusion | flops 2147745792 | bytes 11010048 | tf_op jit(solution)/shard_map/dot_general | solution.py:12
  41.4 0.0 all-gather.5.cloned.1.call-update
  41.4 0.0 reduce-scatter.2.cloned.1.call-start
  42.2 22.0 %all-gather.5.cloned.1.call-done = bf16[256,4096]{1,0:T(8,128)(2,1)} async-done(((bf16[256,1024]{1,0:T(8,128)(2,1)}), bf16[256,4096]{1,0:T(8,128)(2,1)}) %all-gather.5.cloned.1.call-update) | async-done | bytes 2097168 | tf_op jit(solution)/shard_map/all_gather | solution.py:19
  64.2 4.9 %fusion.10 = f32[256,512]{1,0:T(8,128)} fusion(bf16[256,4096]{1,0:T(8,128)(2,1)} %all-gather.5.cloned.1.call-done, bf16[1,512,4096]{2,1,0:T(8,128)(2,1)} %param.5, f32[512]{0:T(512)S(1)} %fusion.13), kind=kOutput, calls=%fused_computation.6 | convolution fusion | flops 1073872896 | bytes 6817792 | tf_op jit(solution)/shard_map/dot_general | solution.py:18
  69.1 0.0 reduce-scatter.2.cloned.1.call-update
  69.1 21.8 %reduce-scatter.2.cloned.1.call-done = f32[64,512]{1,0:T(8,128)} async-done(((f32[256,512]{1,0:T(8,128)}), f32[64,512]{1,0:T(8,128)}) %reduce-scatter.2.cloned.1.call-update) | async-done | bytes 131088 | tf_op jit(solution)/shard_map/reduce_scatter | solution.py:26
  90.9 1.6 %broadcast_multiply_fusion = f32[64,512]{1,0:T(8,128)} fusion(f32[64,512]{1,0:T(8,128)} %reduce-scatter.2.cloned.1.call-done), kind=kLoop, calls=%fused_computation.7 | loop fusion | flops 32768 | bytes 262144 | tf_op jit(solution)/shard_map/mul | solution.py:28
  (1 shorter events, 0.0 us)
Async XLA Ops:
  6.5 27.7 %all-gather.3.cloned.1.call-start = ((), (), s32[]{:S(2)}) async-start(), calls=%async_computation.1 | async-start | bytes 2621440 | tf_op jit(solution)/shard_map/all_gather | solution.py:13
  7.3 56.9 %all-gather.5.cloned.1.call-start = ((), (), s32[]{:S(2)}) async-start(), calls=%async_computation.2 | async-start | bytes 2621440 | tf_op jit(solution)/shard_map/all_gather | solution.py:19
  41.4 49.5 %reduce-scatter.2.cloned.1.call-start = ((), (), s32[]{:S(2)}) async-start(), calls=%async_computation.3 | async-start | bytes 655360 | tf_op jit(solution)/shard_map/reduce_scatter | solution.py:26
Sparse Core Ops, SparseCore 0:
  8.9 25.2 all-gather.2
  41.6 22.5 all-gather.4
  69.3 21.6 reduce-scatter.1
where the time goes:
time: 99.2 us; the launch traced here: 99 us
  waiting for transfers between devices  71.5 us (72%)
  between operations  13.8 us (14%)
  matrix products  12.1 us (12%)
  other arithmetic  1.57 us (2%)
    all_gather x1, waiting for transfers between devices, per_device(): lax.all_gather(query_grads, 'ex', axis=1, tiled=True)[0]  26.9 us
    all_gather x1, waiting for transfers between devices, per_device(): lax.all_gather(column_part, 'ex', axis=1, tiled=True)  22 us
    reduce_scatter x1, waiting for transfers between devices, per_device(): lax.psum_scatter(partial_scores, 'layer', scatter_dimension=0, tiled=True)  21.8 us
    dot_general x1, matrix products, per_device(): lax.dot_general(lax.all_gather(query_grads, 'ex', axis=1, tiled=True)[0],...  7.19 us
    dot_general x1, matrix products, per_device(): lax.dot_general(lax.all_gather(column_part, 'ex', axis=1, tiled=True), tr...  4.91 us
  transfers between devices with their start and end apart: 3, of which 3 were waited for; matrix products, arithmetic and copies ran while one was open for 0% of the time, Pallas kernels for 0%

commit v1 on v0

v1 whole, which is shorter than its diff:
```python
import functools
import math

import jax
import jax.numpy as jnp
from jax import lax
from jax.experimental import pallas as pl
from jax.experimental.pallas import tpu as pltpu
from jax.sharding import PartitionSpec as P

MESH = pl.DeviceIdType.MESH
NT = (((1,), (1,)), ((), ()))
CHUNK = 256


def per_device(query_grads, train_grads, panels, counts):
    train_rows = train_grads[0]
    panel_rows = panels[0]
    column_part = lax.dot_general(
        lax.all_gather(query_grads, "ex", axis=1, tiled=True)[0],
        panel_rows,
        NT,
        preferred_element_type=jnp.float32,
    ).astype(jnp.bfloat16)
    partial_scores = lax.dot_general(
        lax.all_gather(column_part, "ex", axis=1, tiled=True),
        train_rows,
        NT,
        preferred_element_type=jnp.float32,
    )
    alive_mask = (lax.iota(jnp.int32, train_rows.shape[0]) < counts[0]).astype(jnp.float32)
    partial_scores = partial_scores * alive_mask[None, :]
    summed = lax.psum_scatter(partial_scores, "layer", scatter_dimension=0, tiled=True)
    factor = 1.0 / math.sqrt(lax.axis_size("layer") * panel_rows.shape[1])
    return summed * factor


def kernel(layers, q_ref, t_ref, p_ref, o_ref, qbuf, pbuf, tbuf, cbuf, sbuf, sends, lands, loc, psem, send, recv):
    g, e, l = lax.axis_index("groups"), lax.axis_index("ex"), lax.axis_index("layer")
    y, c = e // 2, e % 2
    o = 1 - g
    yo, co = 1 - y, 1 - c
    far = 2 * yo + c
    mate, ypart, xpart = (g, 2 * y + co, l), (g, far, l), (o, e, l)
    half = q_ref.shape[1]
    pair = 2 * half
    depth = p_ref.shape[0]

    def remote(k, src, dst, dev):
        return pltpu.make_async_remote_copy(
            src_ref=src, dst_ref=dst, send_sem=send.at[k], recv_sem=recv.at[k], device_id=dev, device_id_type=MESH
        )

    def qat(yy, hh, cc):
        return qbuf.at[yy, pl.ds(pl.multiple_of(hh * pair + cc * half, half), half), :]

    def rows(hh):
        return pl.ds(pl.multiple_of(hh * pair, pair), pair)

    def cat(ee, yy, hh):
        return cbuf.at[ee, yy, rows(hh), :]

    own = [pltpu.make_async_copy(q_ref.at[h], qat(y, h, c), loc.at[h]) for h in range(2)]
    pcopy = [
        pltpu.make_async_copy(p_ref.at[pl.ds(j * CHUNK, CHUNK), :], pbuf.at[pl.ds(j * CHUNK, CHUNK), :], psem.at[j])
        for j in range(depth // CHUNK)
    ]
    tcopy = pltpu.make_async_copy(t_ref, tbuf, loc.at[2])
    for d in own + pcopy + [tcopy]:
        d.start()

    barrier = pltpu.get_barrier_semaphore()
    zpeers = [(g, e, lax.rem(l + d, layers)) for d in range(1, layers)]
    for dev in [mate, ypart, xpart] + zpeers:
        pl.semaphore_signal(barrier, inc=1, device_id=dev, device_id_type=MESH)
    pl.semaphore_wait(barrier, 2 + layers)

    cp = {}

    def start(k, src, dst, dev):
        cp[k] = remote(k, src, dst, dev)
        cp[k].start()

    start(0, q_ref.at[g], qat(y, g, c), ypart)
    for h in range(2):
        start(1 + h, q_ref.at[h], qat(y, h, c), mate)

    def condition(get_rows, put, first):
        @pl.loop(0, depth // CHUNK)
        def _(j):
            cols = pl.ds(pl.multiple_of(j * CHUNK, CHUNK), CHUNK)
            if first:
                pltpu.make_async_copy(p_ref.at[cols, :], pbuf.at[cols, :], psem.at[j]).wait()
            put(cols, lax.dot_general(get_rows(), pbuf[cols, :], NT, preferred_element_type=jnp.float32))

    for d in own:
        d.wait()
    cp[1].wait_recv()
    cp[2].wait_recv()

    def put_near(cols, v):
        cbuf[e, y, :, cols] = v.astype(jnp.bfloat16)

    condition(lambda: qbuf[y], put_near, True)
    start(8, cat(e, y, g), cat(e, y, g), ypart)
    for h in range(2):
        start(6 + h, cat(e, y, h), cat(e, y, h), mate)

    cp[0].wait_recv()
    start(3, qat(yo, g, c), qat(yo, g, c), mate)
    start(4, qat(yo, g, c), qat(yo, g, c), xpart)
    cp[3].wait_recv()

    def put_far(h):
        def put(cols, v):
            cbuf[e, yo, rows(h), cols] = v.astype(jnp.bfloat16)

        return put

    condition(lambda: qbuf[yo, rows(g), :], put_far(g), False)
    start(9, cat(e, yo, g), cat(e, yo, g), ypart)
    start(10, cat(e, yo, g), cat(e, yo, g), mate)

    cp[8].wait_recv()
    start(12, cat(far, yo, g), cat(far, yo, g), xpart)
    start(13, cat(far, yo, g), cat(far, yo, g), mate)

    cp[4].wait_recv()
    start(5, qat(yo, o, c), qat(yo, o, c), mate)
    cp[5].wait_recv()
    condition(lambda: qbuf[yo, rows(o), :], put_far(o), False)
    start(11, cat(e, yo, o), cat(e, yo, o), mate)

    cp[9].wait_recv()
    start(14, cat(far, y, g), cat(far, y, g), xpart)
    start(15, cat(far, y, g), cat(far, y, g), mate)

    def score(h, base):
        @pl.loop(0, t_ref.shape[0] // CHUNK)
        def _(j):
            slots = pl.ds(pl.multiple_of(j * CHUNK, CHUNK), CHUNK)
            acc = jnp.zeros((2 * pair, CHUNK), jnp.float32)
            for ee in range(4):
                both = jnp.concatenate([cbuf[ee, 0, rows(h), :], cbuf[ee, 1, rows(h), :]], axis=0)
                acc += lax.dot_general(
                    both, tbuf[slots, ee * depth : (ee + 1) * depth], NT, preferred_element_type=jnp.float32
                )
            sbuf[h, :, slots] = acc
            sends[h, :, slots] = acc.astype(sends.dtype)

        for d in range(1, layers):
            dev = zpeers[d - 1]
            start(base + d, sends.at[h, pl.ds(pl.multiple_of(dev[2] * half, half), half), :], lands.at[d - 1, h], dev)

    tcopy.wait()
    for k in (6, 7, 10, 13, 15):
        cp[k].wait_recv()
    score(g, 20)

    cp[12].wait_recv()
    start(16, cat(far, yo, o), cat(far, yo, o), mate)
    cp[14].wait_recv()
    start(17, cat(far, y, o), cat(far, y, o), mate)
    for k in (11, 16, 17):
        cp[k].wait_recv()
    score(o, 20 + layers)

    for d in range(1, layers):
        cp[20 + d].wait_recv()
        cp[20 + layers + d].wait_recv()
    for h in range(2):
        total = sbuf[h, pl.ds(pl.multiple_of(l * half, half), half), :]
        for d in range(1, layers):
            total += lands[d - 1, h].astype(jnp.float32)
        o_ref[h * half : (h + 1) * half, :] = total
    for k in cp:
        cp[k].wait_send()


def per_device_fused(layers, query_grads, train_grads, panels, counts):
    _, block, width = query_grads.shape
    train_rows, panel_rows = train_grads[0], panels[0]
    slots, depth, half = train_rows.shape[0], panel_rows.shape[0], block // 2
    bf16 = jnp.bfloat16
    copies = 20 + 2 * layers
    summed = pl.pallas_call(
        functools.partial(kernel, layers),
        out_shape=jax.ShapeDtypeStruct((block, slots), jnp.float32),
        in_specs=[pl.BlockSpec(memory_space=pl.ANY)] * 3,
        out_specs=pl.BlockSpec(memory_space=pltpu.VMEM),
        scratch_shapes=[
            pltpu.VMEM((2, 4 * half, width), bf16),
            pltpu.VMEM((depth, width), bf16),
            pltpu.VMEM((slots, width), bf16),
            pltpu.VMEM((4, 2, 4 * half, depth), bf16),
            pltpu.VMEM((2, 4 * half, slots), jnp.float32),
            pltpu.VMEM((2, 4 * half, slots), bf16),
            pltpu.VMEM((layers - 1, 2, half, slots), bf16),
            pltpu.SemaphoreType.DMA((3,)),
            pltpu.SemaphoreType.DMA((depth // CHUNK,)),
            pltpu.SemaphoreType.DMA((copies,)),
            pltpu.SemaphoreType.DMA((copies,)),
        ],
        compiler_params=pltpu.CompilerParams(
            collective_id=0, has_side_effects=True, vmem_limit_bytes=48 * 2**20
        ),
        cost_estimate=pl.CostEstimate(
            flops=2 * 4 * block * width * (depth + slots), bytes_accessed=2 * width * (block + depth + slots),
            transcendentals=0,
        ),
    )(query_grads.reshape(2, half, width), train_rows, panel_rows)
    alive_mask = (lax.iota(jnp.int32, slots) < counts[0]).astype(jnp.float32)
    factor = 1.0 / math.sqrt(layers * width)
    return summed * (alive_mask * factor)[None, :]


def solution(mesh):
    in_specs = (
        P("layer", "ex", None),
        P("layer", ("groups", "ex"), None),
        P("layer", "ex", None),
        P(("groups", "ex")),
    )
    out_specs = P("layer", ("groups", "ex"))
    shape = dict(mesh.shape)
    body = per_device
    if shape == {"groups": 2, "ex": 4, "layer": 4}:
        body = functools.partial(per_device_fused, shape["layer"])
    return jax.shard_map(body, mesh=mesh, in_specs=in_specs, out_specs=out_specs, check_vma=False)
```

time: 99.2 us -> 39.3 us (0.40)
  waiting for transfers between devices: 71.5 us -> 0 us
  Pallas kernels: 0 us -> 34.5 us
  between operations: 13.8 us -> 0.68 us
  matrix products: 12.1 us -> 0 us
  local copies, waits for them, and re-layouts: 0 us -> 3.22 us
    all_gather x2 -> x0, waiting for transfers between devices: 49 us -> none  [the longest x1 26.9 us: per_device(): lax.all_gather(query_grads, 'ex', axis=1, tiled=True)[0]]
    pallas_call x0 -> x1, Pallas kernels: none -> 34.5 us  [per_device_fused(): pl.pallas_call(functools.partial(kernel, layers), out_shape=jax.ShapeDtyp...]
    reduce_scatter x1 -> x0, waiting for transfers between devices: 21.8 us -> none  [per_device(): lax.psum_scatter(partial_scores, 'layer', scatter_dimension=0, tiled=True)]
    dot_general x2 -> x0, matrix products: 12.1 us -> none  [the longest x1 7.19 us: per_device(): lax.dot_general(lax.all_gather(query_grads, 'ex', axis=1, tiled=True)[0],...]
    unnamed x0 -> x4, local copies, waits for them, and re-layouts: none -> 3.22 us
  transfers between devices with their start and end apart: 3 -> 0, of which waited for: 3 -> 0; matrix products, arithmetic and copies ran while one was open for 0% -> 0% of each run, Pallas kernels for 0% -> 0%
where the time goes in v1:
time: 39.3 us; the launch traced here: 39.1 us
  Pallas kernels  34.5 us (88%)
  local copies, waits for them, and re-layouts  3.22 us (8%)
  between operations  0.68 us (2%)
  other arithmetic  0.67 us (2%)
    pallas_call x1, Pallas kernels, per_device_fused(): pl.pallas_call(functools.partial(kernel, layers), out_shape=jax.ShapeDtyp...  34.5 us
    unnamed x4, local copies, waits for them, and re-layouts  3.22 us

profile of v1, /device:TPU:0, one launch (start us, length us, event | category | flops | bytes accessed | tf_op | source)
XLA Modules:
  0.0 39.1 jit_solution(453211065402722251)
XLA Ops:
  0.7 0.0 copy-start
  0.7 2.2 %copy-done = bf16[1,512,4096]{2,1,0:T(8,128)(2,1)S(1)} copy-done((bf16[1,512,4096]{2,1,0:T(8,128)(2,1)S(1)}, bf16[1,512,4096]{2,1,0:T(8,128)(2,1)}, u32[]{:S(2)}) %copy-start) | copy-done | bytes 4194328
  2.9 0.0 copy-start.1
  2.9 1.0 %copy-done.1 = bf16[1,64,4096]{2,1,0:T(8,128)(2,1)S(1)} copy-done((bf16[1,64,4096]{2,1,0:T(8,128)(2,1)S(1)}, bf16[1,64,4096]{2,1,0:T(8,128)(2,1)}, u32[]{:S(2)}) %copy-start.1) | copy-done | bytes 524312
  3.9 34.5 %shard_map.46 = f32[64,512]{1,0:T(8,128)S(1)} custom-call(bf16[2,32,4096]{2,1,0:T(8,128)(2,1)S(1)} %bitcast.6, bf16[512,4096]{1,0:T(8,128)(2,1)S(1)} %bitcast.5, bf16[1024,4096]{1,0:T(8,128)(2,1)} %bitcast.7), custom_call_target="tpu_custom_call" | custom-call | flops 3221225472 | bytes 13107200 | tf_op jit(solution)/shard_map/pallas_call | solution.py:186
  38.4 0.7 %broadcast_multiply_fusion = f32[64,512]{1,0:T(8,128)} fusion(f32[64,512]{1,0:T(8,128)S(1)} %shard_map.46, f32[512]{0:T(512)S(1)} %fusion), kind=kLoop, calls=%fused_computation | loop fusion | flops 32768 | bytes 264192 | tf_op jit(solution)/shard_map/mul | solution.py:214
  (1 shorter events, 0.0 us)
Async XLA Ops:
  0.7 2.2 %copy-start = (bf16[1,512,4096]{2,1,0:T(8,128)(2,1)S(1)}, bf16[1,512,4096]{2,1,0:T(8,128)(2,1)}, u32[]{:S(2)}) copy-start(bf16[1,512,4096]{2,1,0:T(8,128)(2,1)} %param.5) | copy-start | bytes 12582916
  2.9 1.0 %copy-start.1 = (bf16[1,64,4096]{2,1,0:T(8,128)(2,1)S(1)}, bf16[1,64,4096]{2,1,0:T(8,128)(2,1)}, u32[]{:S(2)}) copy-start(bf16[1,64,4096]{2,1,0:T(8,128)(2,1)} %param.4) | copy-start | bytes 1572868

commit v2 on v1

v2 whole, which is shorter than its diff:
```python
import functools
import math

import jax
import jax.numpy as jnp
from jax import lax
from jax.experimental import pallas as pl
from jax.experimental.pallas import tpu as pltpu
from jax.sharding import PartitionSpec as P

MESH = pl.DeviceIdType.MESH
NT = (((1,), (1,)), ((), ()))
CHUNK = 512
SLOTS = 256


def per_device(query_grads, train_grads, panels, counts):
    train_rows = train_grads[0]
    panel_rows = panels[0]
    column_part = lax.dot_general(
        lax.all_gather(query_grads, "ex", axis=1, tiled=True)[0],
        panel_rows,
        NT,
        preferred_element_type=jnp.float32,
    ).astype(jnp.bfloat16)
    partial_scores = lax.dot_general(
        lax.all_gather(column_part, "ex", axis=1, tiled=True),
        train_rows,
        NT,
        preferred_element_type=jnp.float32,
    )
    alive_mask = (lax.iota(jnp.int32, train_rows.shape[0]) < counts[0]).astype(jnp.float32)
    partial_scores = partial_scores * alive_mask[None, :]
    summed = lax.psum_scatter(partial_scores, "layer", scatter_dimension=0, tiled=True)
    factor = 1.0 / math.sqrt(lax.axis_size("layer") * panel_rows.shape[1])
    return summed * factor


def kernel(layers, q_ref, t_ref, p_ref, o_ref, qbuf, pbuf, tbuf, cbuf, sbuf, sends, lands, loc, psem, send, recv):
    g, e, l = lax.axis_index("groups"), lax.axis_index("ex"), lax.axis_index("layer")
    y, c = e // 2, e % 2
    o = 1 - g
    yo, co = 1 - y, 1 - c
    far = 2 * yo + c
    mate, ypart, xpart = (g, 2 * y + co, l), (g, far, l), (o, e, l)
    half = q_ref.shape[1]
    pair, quarter = 2 * half, half // 2
    depth = p_ref.shape[0]

    def remote(k, src, dst, dev):
        return pltpu.make_async_remote_copy(
            src_ref=src, dst_ref=dst, send_sem=send.at[k], recv_sem=recv.at[k], device_id=dev, device_id_type=MESH
        )

    def qat(yy, hh, cc):
        return qbuf.at[yy, pl.ds(pl.multiple_of(hh * pair + cc * half, half), half), :]

    def rows(hh):
        return pl.ds(pl.multiple_of(hh * pair, pair), pair)

    def cat(ee, yy, hh):
        return cbuf.at[ee, yy, rows(hh), :]

    def piece(ref, s):
        return ref.at[pl.ds(s * quarter, quarter), :]

    def part(ref, s):
        return ref.at[:, pl.ds(s * CHUNK, CHUNK)]

    parts = range(depth // CHUNK)
    own = [pltpu.make_async_copy(q_ref.at[h], qat(y, h, c), loc.at[h]) for h in range(2)]
    pcopy = [
        pltpu.make_async_copy(p_ref.at[pl.ds(j * CHUNK, CHUNK), :], pbuf.at[pl.ds(j * CHUNK, CHUNK), :], psem.at[j])
        for j in parts
    ]
    tcopy = pltpu.make_async_copy(t_ref, tbuf, loc.at[2])
    for d in own + pcopy:
        d.start()

    barrier = pltpu.get_barrier_semaphore()
    zpeers = [(g, e, lax.rem(l + d, layers)) for d in range(1, layers)]
    for dev in zpeers + [ypart, xpart, mate]:
        pl.semaphore_signal(barrier, inc=1, device_id=dev, device_id_type=MESH)
    pl.semaphore_wait(barrier, 2 + layers)

    cp = {}

    def start(name, src, dst, dev):
        k = len(cp)
        cp[name] = remote(k, src, dst, dev)
        cp[name].start()

    def arrived(*names):
        for name in names:
            cp[name].wait_recv()

    for s in range(2):
        start(("qy", s), piece(q_ref.at[g], s), piece(qat(y, g, c), s), ypart)
    for h in range(2):
        start(("qm", h), q_ref.at[h], qat(y, h, c), mate)
    tcopy.start()

    def condition(j, q, yy, where):
        cols = pl.ds(j * CHUNK, CHUNK)
        v = lax.dot_general(q, pbuf[cols, :], NT, preferred_element_type=jnp.float32)
        cbuf[e, yy, where, cols] = v.astype(jnp.bfloat16)

    def hand_on_queries(s):
        arrived(("qy", s))
        got = piece(qat(yo, g, c), s)
        start(("qym", s), got, got, mate)
        start(("qyx", s), got, got, xpart)

    for d in own:
        d.wait()
    arrived(("qm", 0), ("qm", 1))
    for j in parts:
        pcopy[j].wait()
        condition(j, qbuf[y], y, slice(None))
        if j == 0:
            hand_on_queries(0)
    start("ay", cat(e, y, g), cat(e, y, g), ypart)
    hand_on_queries(1)
    for h in range(2):
        start(("am", h), cat(e, y, h), cat(e, y, h), mate)

    arrived(("qym", 0), ("qym", 1))
    for j in parts:
        condition(j, qbuf[yo, rows(g), :], yo, rows(g))
        start(("by", j), part(cat(e, yo, g), j), part(cat(e, yo, g), j), ypart)
        start(("bm", j), part(cat(e, yo, g), j), part(cat(e, yo, g), j), mate)
        if j == 0:
            arrived("ay")
            start("ayx", cat(far, yo, g), cat(far, yo, g), xpart)
            start("aym", cat(far, yo, g), cat(far, yo, g), mate)

    for s in range(2):
        arrived(("qyx", s))
        start(("qxm", s), piece(qat(yo, o, c), s), piece(qat(yo, o, c), s), mate)
    arrived(("qxm", 0), ("qxm", 1))
    for j in parts:
        condition(j, qbuf[yo, rows(o), :], yo, rows(o))
        start(("cm", j), part(cat(e, yo, o), j), part(cat(e, yo, o), j), mate)
        if j == 0:
            for i in parts:
                arrived(("by", i))
                got = part(cat(far, y, g), i)
                start(("byx", i), got, got, xpart)
                start(("bym", i), got, got, mate)

    arrived("ayx")
    start("axm", cat(far, yo, o), cat(far, yo, o), mate)

    def score(h, owners, first, last):
        @pl.loop(0, t_ref.shape[0] // SLOTS)
        def _(j):
            slots = pl.ds(pl.multiple_of(j * SLOTS, SLOTS), SLOTS)
            acc = None if first else sbuf[h, :, slots]
            for ee in owners:
                both = jnp.concatenate([cbuf[ee, 0, rows(h), :], cbuf[ee, 1, rows(h), :]], axis=0)
                span = pl.ds(pl.multiple_of(ee * depth, depth), depth)
                term = lax.dot_general(both, tbuf[slots, span], NT, preferred_element_type=jnp.float32)
                acc = term if acc is None else acc + term
            sbuf[h, :, slots] = acc
            if last:
                sends[h, :, slots] = acc.astype(sends.dtype)

        if last:
            for d in range(1, layers):
                dev = zpeers[d - 1]
                mine = pl.ds(pl.multiple_of(dev[2] * half, half), half)
                start(("z", first, d), sends.at[h, mine, :], lands.at[d - 1, h], dev)

    near, away = [2 * y, 2 * y + 1], [2 * yo, 2 * yo + 1]
    tcopy.wait()
    arrived(("am", 0), ("am", 1), "aym")
    for i in parts:
        arrived(("bm", i), ("bym", i))
    score(g, near + away, True, True)

    for i in parts:
        if i == len(parts) - 1:
            for j in parts:
                arrived(("cm", j))
            score(o, near, True, False)
        arrived(("byx", i))
        got = part(cat(far, y, o), i)
        start(("bxm", i), got, got, mate)
    arrived("axm")
    for i in parts:
        arrived(("bxm", i))
    score(o, away, False, True)

    for d in range(1, layers):
        arrived(("z", True, d), ("z", False, d))
    for h in range(2):
        total = sbuf[h, pl.ds(pl.multiple_of(l * half, half), half), :]
        for d in range(1, layers):
            total += lands[d - 1, h].astype(jnp.float32)
        o_ref[h * half : (h + 1) * half, :] = total
    for name in cp:
        cp[name].wait_send()


def per_device_fused(layers, query_grads, train_grads, panels, counts):
    _, block, width = query_grads.shape
    train_rows, panel_rows = train_grads[0], panels[0]
    slots, depth, half = train_rows.shape[0], panel_rows.shape[0], block // 2
    bf16 = jnp.bfloat16
    copies = 40 + 2 * layers
    summed = pl.pallas_call(
        functools.partial(kernel, layers),
        out_shape=jax.ShapeDtypeStruct((block, slots), jnp.float32),
        in_specs=[pl.BlockSpec(memory_space=pl.ANY)] * 3,
        out_specs=pl.BlockSpec(memory_space=pltpu.VMEM),
        scratch_shapes=[
            pltpu.VMEM((2, 4 * half, width), bf16),
            pltpu.VMEM((depth, width), bf16),
            pltpu.VMEM((slots, width), bf16),
            pltpu.VMEM((4, 2, 4 * half, depth), bf16),
            pltpu.VMEM((2, 4 * half, slots), jnp.float32),
            pltpu.VMEM((2, 4 * half, slots), bf16),
            pltpu.VMEM((layers - 1, 2, half, slots), bf16),
            pltpu.SemaphoreType.DMA((3,)),
            pltpu.SemaphoreType.DMA((depth // CHUNK,)),
            pltpu.SemaphoreType.DMA((copies,)),
            pltpu.SemaphoreType.DMA((copies,)),
        ],
        compiler_params=pltpu.CompilerParams(
            collective_id=0, has_side_effects=True, vmem_limit_bytes=60 * 2**20
        ),
        cost_estimate=pl.CostEstimate(
            flops=2 * 4 * block * width * (depth + slots), bytes_accessed=2 * width * (block + depth + slots),
            transcendentals=0,
        ),
    )(query_grads.reshape(2, half, width), train_rows, panel_rows)
    alive_mask = (lax.iota(jnp.int32, slots) < counts[0]).astype(jnp.float32)
    factor = 1.0 / math.sqrt(layers * width)
    return summed * (alive_mask * factor)[None, :]


def solution(mesh):
    in_specs = (
        P("layer", "ex", None),
        P("layer", ("groups", "ex"), None),
        P("layer", "ex", None),
        P(("groups", "ex")),
    )
    out_specs = P("layer", ("groups", "ex"))
    shape = dict(mesh.shape)
    body = per_device
    if shape == {"groups": 2, "ex": 4, "layer": 4}:
        body = functools.partial(per_device_fused, shape["layer"])
    return jax.shard_map(body, mesh=mesh, in_specs=in_specs, out_specs=out_specs, check_vma=False)
```

time: 39.3 us -> 35.2 us (0.90)
  local copies, waits for them, and re-layouts: 3.22 us -> 0 us
  Pallas kernels: 34.5 us -> 32.8 us
  other arithmetic: 0.67 us -> 1.58 us
    unnamed x4 -> x0, local copies, waits for them, and re-layouts: 3.22 us -> none
    pallas_call x1, Pallas kernels: 34.5 us -> 32.8 us  [per_device_fused(): pl.pallas_call(functools.partial(kernel, layers), out_shape=jax.ShapeDtyp...]
    mul x2, other arithmetic: 0.67 us -> 1.58 us  [per_device_fused(): return summed * (alive_mask * factor)[None, :]]
where the time goes in v2:
time: 35.2 us; the launch traced here: 35.1 us
  Pallas kernels  32.8 us (93%)
  other arithmetic  1.58 us (4%)
  between operations  0.67 us (2%)
    pallas_call x1, Pallas kernels, per_device_fused(): pl.pallas_call(functools.partial(kernel, layers), out_shape=jax.ShapeDtyp...  32.8 us
    mul x2, other arithmetic, per_device_fused(): return summed * (alive_mask * factor)[None, :]  1.58 us

profile of v2, /device:TPU:0, one launch (start us, length us, event | category | flops | bytes accessed | tf_op | source)
XLA Modules:
  0.0 35.1 jit_solution(4267433412748656828)
XLA Ops:
  0.7 32.8 %shard_map.46 = f32[64,512]{1,0:T(8,128)} custom-call(bf16[2,32,4096]{2,1,0:T(8,128)(2,1)} %bitcast.7, bf16[512,4096]{1,0:T(8,128)(2,1)} %bitcast.6, bf16[1024,4096]{1,0:T(8,128)(2,1)} %bitcast.5), custom_call_target="tpu_custom_call" | custom-call | flops 3221225472 | bytes 13107200 | tf_op jit(solution)/shard_map/pallas_call | solution.py:211
  33.5 1.6 %broadcast_multiply_fusion = f32[64,512]{1,0:T(8,128)} fusion(f32[64,512]{1,0:T(8,128)} %shard_map.46, f32[512]{0:T(512)S(1)} %fusion), kind=kLoop, calls=%fused_computation | loop fusion | flops 32768 | bytes 264192 | tf_op jit(solution)/shard_map/mul | solution.py:239
  (1 shorter events, 0.0 us)

commit v3 on v2

--- a/solution.py
+++ b/solution.py
@@ -117,10 +117,9 @@
     for j in parts:
         pcopy[j].wait()
         condition(j, qbuf[y], y, slice(None))
-        if j == 0:
-            hand_on_queries(0)
     start("ay", cat(e, y, g), cat(e, y, g), ypart)
-    hand_on_queries(1)
+    for s in range(2):
+        hand_on_queries(s)
     for h in range(2):
         start(("am", h), cat(e, y, h), cat(e, y, h), mate)
 

time: 35.2 us -> 35.4 us (level)
  no operation moved by 1% of the time
where the time goes in v3:
time: 35.4 us; the launch traced here: 35.3 us
  Pallas kernels  33 us (93%)
  other arithmetic  1.58 us (4%)
  between operations  0.67 us (2%)
    pallas_call x1, Pallas kernels, per_device_fused(): pl.pallas_call(functools.partial(kernel, layers), out_shape=jax.ShapeDtyp...  33 us
    mul x2, other arithmetic, per_device_fused(): return summed * (alive_mask * factor)[None, :]  1.58 us

profile of v3, /device:TPU:0, one launch (start us, length us, event | category | flops | bytes accessed | tf_op | source)
XLA Modules:
  0.0 35.3 jit_solution(15547896188225132944)
XLA Ops:
  0.7 33.0 %shard_map.46 = f32[64,512]{1,0:T(8,128)} custom-call(bf16[2,32,4096]{2,1,0:T(8,128)(2,1)} %bitcast.7, bf16[512,4096]{1,0:T(8,128)(2,1)} %bitcast.6, bf16[1024,4096]{1,0:T(8,128)(2,1)} %bitcast.5), custom_call_target="tpu_custom_call" | custom-call | flops 3221225472 | bytes 13107200 | tf_op jit(solution)/shard_map/pallas_call | solution.py:210
  33.7 1.6 %broadcast_multiply_fusion = f32[64,512]{1,0:T(8,128)} fusion(f32[64,512]{1,0:T(8,128)} %shard_map.46, f32[512]{0:T(512)S(1)} %fusion), kind=kLoop, calls=%fused_computation | loop fusion | flops 32768 | bytes 264192 | tf_op jit(solution)/shard_map/mul | solution.py:238
  (1 shorter events, 0.0 us)

commit v4 on v2

--- a/solution.py
+++ b/solution.py
@@ -102,8 +102,8 @@
 
     def condition(j, q, yy, where):
         cols = pl.ds(j * CHUNK, CHUNK)
-        v = lax.dot_general(q, pbuf[cols, :], NT, preferred_element_type=jnp.float32)
-        cbuf[e, yy, where, cols] = v.astype(jnp.bfloat16)
+        v = lax.dot_general(pbuf[cols, :], q, NT, preferred_element_type=jnp.float32)
+        cbuf[e, yy, where, cols] = v.astype(jnp.bfloat16).T
 
     def hand_on_queries(s):
         arrived(("qy", s))

time: 35.2 us -> 38.4 us (1.091)
  Pallas kernels: 32.8 us -> 36 us
    pallas_call x1, Pallas kernels: 32.8 us -> 36 us  [per_device_fused(): pl.pallas_call(functools.partial(kernel, layers), out_shape=jax.ShapeDtyp...]
where the time goes in v4:
time: 38.4 us; the launch traced here: 38.2 us
  Pallas kernels  36 us (94%)
  other arithmetic  1.58 us (4%)
  between operations  0.67 us (2%)
    pallas_call x1, Pallas kernels, per_device_fused(): pl.pallas_call(functools.partial(kernel, layers), out_shape=jax.ShapeDtyp...  36 us
    mul x2, other arithmetic, per_device_fused(): return summed * (alive_mask * factor)[None, :]  1.58 us

profile of v4, /device:TPU:0, one launch (start us, length us, event | category | flops | bytes accessed | tf_op | source)
XLA Modules:
  0.0 38.2 jit_solution(2511799575311532769)
XLA Ops:
  0.7 36.0 %shard_map.46 = f32[64,512]{1,0:T(8,128)} custom-call(bf16[2,32,4096]{2,1,0:T(8,128)(2,1)} %bitcast.7, bf16[512,4096]{1,0:T(8,128)(2,1)} %bitcast.6, bf16[1024,4096]{1,0:T(8,128)(2,1)} %bitcast.5), custom_call_target="tpu_custom_call" | custom-call | flops 3221225472 | bytes 13107200 | tf_op jit(solution)/shard_map/pallas_call | solution.py:211
  36.6 1.6 %broadcast_multiply_fusion = f32[64,512]{1,0:T(8,128)} fusion(f32[64,512]{1,0:T(8,128)} %shard_map.46, f32[512]{0:T(512)S(1)} %fusion), kind=kLoop, calls=%fused_computation | loop fusion | flops 32768 | bytes 264192 | tf_op jit(solution)/shard_map/mul | solution.py:239
  (1 shorter events, 0.0 us)
